TPU v7x, 128 devices: a whole 4x4x4 slice. The times are simulated.
128 devices in a mesh: section: 2 (over x_lo), dp: 64 (over z, y, x_hi, core).
Axes of the slice: x: 4 (x_hi: 2, x_lo: 2; x = x_hi * 2 + x_lo), y: 4, z: 4, core: 2. Of those that a mesh axis runs over, the one named last changes fastest.
Arguments:
- inputs: bfloat16 [2, 4, 10240, 4096], P('section', None, 'dp'), may hold values from -40 to 40
- query_grads: bfloat16 [2, 4, 10240, 4096], P('section', None, 'dp'), may hold values from -40 to 40
- plan: int32 [2, 64, 2], P('section'), may hold values from 0 to 3, as said below
Outputs:
- inverses: bfloat16 [2, 64, 128, 128], P('section')
Inputs may be any that keep to these rules, and one draw needn't show every extreme that they name: plan[s, f, 0] is the segment that damps and inverts factor f of segment s (it may be s itself); within one segment's 64 factors no segment is named more than 32 times, and in every segment's block some segment is named exactly 32 times. plan[s, f, 1] is the last micro-batch whose statistics enter that factor.
All inputs are finite; a program needn't handle non-finite values.
Results may differ from a plain program's by a relative error of at most 0.001.
Values may be sent and summed in bfloat16 or wider, within the bound.
A program may use at most 128 MiB of HBM per device.

v0:
```python
import jax
import jax.numpy as jnp
from jax import lax
from jax.sharding import PartitionSpec as P

HEAD = 128
MOST = 32


DAMPING = 0.3


def invert(factors):
    block_size = factors.shape[-1]
    identity = jnp.eye(block_size, dtype=jnp.float32)
    damped = factors + DAMPING * identity
    lower_factor = jnp.linalg.cholesky(damped)
    right_side = jnp.broadcast_to(identity, damped.shape)
    halfway = lax.linalg.triangular_solve(lower_factor, right_side, left_side=True, lower=True)
    inverse = lax.linalg.triangular_solve(
        lower_factor, halfway, left_side=True, lower=True, transpose_a=True
    )
    return inverse.astype(jnp.bfloat16)


def slot_weights(newest, batches, rows_all):
    indices = jnp.arange(batches, dtype=jnp.int32)
    included = (indices[None, :] <= newest[:, None]).astype(jnp.float32)
    return included / (rows_all * (newest[:, None] + 1).astype(jnp.float32))


def block_grams(blocks, weights):
    gram_blocks = jnp.einsum("mtfi,mtfj->mfij", blocks, blocks, preferred_element_type=jnp.float32)
    return jnp.einsum("fm,mfij->fij", weights, gram_blocks, precision=lax.Precision.HIGHEST)


def route_table(destination, segments, capacity):
    segment_ids = jnp.arange(segments, dtype=jnp.int32)
    dest_marks = (destination[:, None] == segment_ids[None, :]).astype(jnp.int32)
    before = jnp.cumsum(dest_marks, axis=0) - dest_marks
    position = jnp.sum(before * dest_marks, axis=1)
    target = destination * capacity + position
    slot_ids = jnp.arange(segments * capacity, dtype=jnp.int32)
    return slot_ids[:, None] == target[None, :]


def offload(factors, destination, capacity):
    segments = lax.axis_size("section")
    factor_count = factors.shape[0]
    block_size = factors.shape[-1]
    slot_table = route_table(destination, segments, capacity)
    flattened = factors.reshape(factor_count, block_size * block_size)
    packed = jnp.dot(slot_table.astype(jnp.float32), flattened, precision=lax.Precision.HIGHEST)
    packed = packed.reshape(segments, capacity, block_size, block_size)
    returned = lax.all_to_all(
        invert(lax.all_to_all(packed, "section", split_axis=0, concat_axis=0, tiled=True)),
        "section",
        split_axis=0,
        concat_axis=0,
        tiled=True,
    )
    returned = returned.reshape(segments * capacity, block_size * block_size)
    unpacked = jnp.dot(
        slot_table.T.astype(jnp.bfloat16), returned, preferred_element_type=jnp.float32
    )
    return unpacked.astype(jnp.bfloat16).reshape(factor_count, block_size, block_size)


def shards(inputs, query_grads, plan):
    batches = inputs.shape[1]
    tokens = inputs.shape[2]
    columns = inputs.shape[3]
    head_count = columns // HEAD
    members = lax.axis_size("dp")
    routing = plan[0]
    weights = slot_weights(routing[:, 1], batches, tokens * members)
    in_blocks = inputs[0].reshape(batches, tokens, head_count, HEAD)
    grad_blocks = query_grads[0].reshape(batches, tokens, head_count, HEAD)
    local_term = jnp.concatenate(
        (
            block_grams(in_blocks, weights[:head_count]),
            block_grams(grad_blocks, weights[head_count:]),
        ),
        axis=0,
    )
    factors = lax.psum(local_term, "dp")
    result = offload(factors, routing[:, 0], MOST)
    return result[None]


def solution(mesh):
    in_specs = (
        P("section", None, "dp", None),
        P("section", None, "dp", None),
        P("section", None, None),
    )
    out_specs = P("section", None, None, None)
    return jax.shard_map(shards, mesh=mesh, in_specs=in_specs, out_specs=out_specs, check_vma=False)
```

profile of v0, /device:TPU:1, one launch (start us, length us, event | category | flops | bytes accessed | tf_op | source)
XLA Modules:
  0.0 2245.5 jit_solution(6468878160553453280)
XLA Ops:
  6.5 0.8 slice_bitcast_fusion
  7.3 0.7 multiply_bitcast_fusion
  8.1 4.1 copy.30
  12.2 7.1 fusion.4
  19.3 4.1 copy.29
  23.4 3.9 fusion.6
  27.3 25.1 %fusion = f32[32,1,128,128]{3,1,2,0:T(1,128)S(1)} fusion(f32[32,4,1,1]{1,2,3,0:T(1,128)S(1)} %bitcast.83, f32[4,32,128,128]{3,2,1,0:T(8,128)} %fusion.4), kind=kOutput, calls=%fused_computation.1 | convolution fusion | flops 25165824 | bytes 10486272 | tf_op jit(solution)/shard_map/fm,mfij->fij/dot_general | solution.py:34
  52.3 18.5 fusion.2
  70.9 0.3 pad_maximum_fusion
  71.2 4.4 copy_bitcast_fusion
  75.7 0.1 reduce_window_sum.11
  75.8 0.2 select_reduce_fusion.1
  75.9 0.3 copy-done.2
  76.2 650.2 %all-reduce.2.cloned.1.call-done = f32[128,128,64]{1,2,0:T(8,128)} async-done(((f32[128,128,64]{1,2,0:T(8,128)}), f32[128,128,64]{1,2,0:T(8,128)}) %all-reduce.2.cloned.1.call-update) | async-done | bytes 4194320 | tf_op jit(solution)/shard_map/psum | solution.py:86
  726.5 6.5 fusion.13
  733.0 5.3 copy.16
  738.3 5.6 all-to-all-start
  744.1 46.3 %all-to-all-done = f32[2,32,128,128]{2,3,1,0:T(8,128)} async-done(((f32[2,32,128,128]{2,3,1,0:T(8,128)}), f32[2,32,128,128]{2,3,1,0:T(8,128)}, u32[]{:S(2)}, u32[]{:S(2)}) %all-to-all-start) | async-done | bytes 4194336 | tf_op jit(solution)/shard_map/all_to_all | solution.py:56
  790.5 4.7 broadcast_add_fusion
  795.2 5.8 copy.18
  801.0 6.7 fusion.12
  807.7 752.0 %custom-call.9 = f32[2,32,128,128]{3,2,1,0:T(8,128)} custom-call(f32[2,32,128,128]{3,2,1,0:T(8,128)} %fusion.12), custom_call_target="Cholesky" | custom-call | tf_op jit(solution)/shard_map/jit(cholesky)/cholesky | solution.py:17
  1559.7 2.9 select_reduce_fusion
  1562.6 0.1 compare_reduce_fusion
  1562.7 0.4 copy-done
  1563.1 2.5 select_bitcast_fusion
  1565.6 630.2 %custom-call.10 = f32[2,32,1,128,128]{3,4,2,1,0:T(8,128)} custom-call(f32[2,32,1,128,128]{4,3,2,1,0:T(8,128)} %select_bitcast_fusion), custom_call_target="InvertDiagBlocksLowerTriangular" | custom-call | tf_op jit(solution)/shard_map/triangular_solve | solution.py:20
  2195.8 8.9 fusion.10
  2204.7 4.5 fusion.18
  2209.2 25.6 %all_to_all.10 = bf16[2,32,128,128]{3,2,1,0:T(8,128)(2,1)S(1)} all-to-all(bf16[2,32,128,128]{3,2,1,0:T(8,128)(2,1)S(1)} %fusion.18), channel_id=1, replica_groups=mesh['section'=2,'dp'=64] {'section'}, dimensions={0} | all-to-all | bytes 4194304 | tf_op jit(solution)/shard_map/all_to_all | solution.py:55
  2234.8 1.7 fusion.21
  2236.5 1.9 copy.33
  (16 shorter events, 0.3 us)
Async XLA Ops:
  6.5 720.0 %all-reduce.2.cloned.1.call-start = ((), (), s32[]{:S(2)}) async-start(), calls=%async_computation.2 | async-start | bytes 8388608 | tf_op jit(solution)/shard_map/psum | solution.py:86
  75.6 0.7 copy-start.2
  738.3 52.1 %all-to-all-start = ((f32[2,32,128,128]{2,3,1,0:T(8,128)}), f32[2,32,128,128]{2,3,1,0:T(8,128)}, u32[]{:S(2)}, u32[]{:S(2)}) async-start(f32[2,32,128,128]{2,3,1,0:T(8,128)} %copy.16), calls=%async_computation | async-start | bytes 8388608 | tf_op jit(solution)/shard_map/all_to_all | solution.py:56
  1559.7 3.4 copy-start
  2195.8 8.9 copy-start.1
Sparse Core Ops, SparseCore 0:
  75.7 650.7 all-reduce.1
where the time goes:
time: 2250 us
  other arithmetic  1400 us (62%)
  waiting for transfers between devices  697 us (31%)
  matrix products  76.1 us (3%)
  local copies, waits for them, and re-layouts  27.2 us (1%)
  blocking collectives  25.6 us (1%)
    another operation x4, other arithmetic, invert(): lower_factor = jnp.linalg.cholesky(damped)  755 us
    psum x1, waiting for transfers between devices, shards(): factors = lax.psum(local_term, 'dp')  650 us
    another operation x3, other arithmetic, invert(): lax.linalg.triangular_solve(lower_factor, halfway, left_side=True, lower=...  633 us
    all_to_all x1, waiting for transfers between devices, offload(): lax.all_to_all(packed, 'section', split_axis=0, concat_axis=0, tiled=True)  46.3 us
  transfers between devices with their start and end apart: 2, of which 2 were waited for; matrix products, arithmetic and copies ran while one was open for 0% of the time, Pallas kernels for 0%

commit v1 on v0

v1 whole, which is shorter than its diff:
```python
import functools

import jax
import jax.numpy as jnp
from jax import lax
from jax.experimental import pallas as pl
from jax.experimental.pallas import tpu as pltpu
from jax.sharding import PartitionSpec as P

HEAD = 128
DAMPING = 0.3
MICRO = 4
PAIRS = 16
PACK = 136
CUT = 64
MESH = pl.DeviceIdType.MESH

ORDER = (
    (2, 2), (2, 1), (1, 2), (2, 3),
    (3, 2), (1, 1), (1, 3), (3, 1),
    (3, 3), (2, 0), (0, 2), (1, 0),
    (0, 1), (3, 0), (0, 3), (0, 0),
)
SLOT = {offset: slot for slot, offset in enumerate(ORDER)}
GROUP = 4


def split3(x):
    high = x.astype(jnp.bfloat16)
    x = x - high.astype(jnp.float32)
    middle = x.astype(jnp.bfloat16)
    x = x - middle.astype(jnp.float32)
    return high, middle, x.astype(jnp.bfloat16)


def product(a, b):
    ah, am, al = split3(a)
    bh, bm, bl = split3(b)
    left = jnp.concatenate([ah, ah, am, ah, al, am], 0)
    right = jnp.concatenate([bh, bm, bh, bl, bh, bm], 0)
    return lax.dot_general(left, right, (((0,), (0,)), ((), ())), preferred_element_type=jnp.float32)


def spread(x):
    return jnp.broadcast_to(x, (8, HEAD))


def invert(matrix):
    lane = lax.broadcasted_iota(jnp.int32, (8, HEAD), 1)
    sub = lax.broadcasted_iota(jnp.int32, (8, HEAD), 0)
    rows = [matrix[8 * g : 8 * g + 8, :] for g in range(16)]
    for g in range(16):
        base = 8 * g
        panel = rows[g]
        inside = (lane >= base) & (lane < base + 8)
        columns = [spread(panel[:, base + j : base + j + 1]) for j in range(8)]
        a = {(i, j): spread(columns[j][i : i + 1, :]) for i in range(8) for j in range(i, 8)}
        start = jnp.where(inside, jnp.where(lane - base == sub, 1.0, 0.0), panel)
        w = [spread(start[j : j + 1, :]) for j in range(8)]
        more = g + 1 < 16
        if more:
            following = rows[g + 1]
            c = [spread(following[:, base + j : base + j + 1]) for j in range(8)]
        low = {}
        inverse_d = [None] * 8
        for i in (0, 2, 4, 6):
            p, q, r = a[i, i], a[i, i + 1], a[i + 1, i + 1]
            d0 = 1.0 / p
            d1 = p * (1.0 / (p * r - q * q))
            l10 = q * d0
            inverse_d[i], inverse_d[i + 1] = d0, d1
            low[i + 1, i] = l10
            e0 = {j: a[i, j] for j in range(i + 2, 8)}
            e1 = {j: a[i + 1, j] - l10 * a[i, j] for j in range(i + 2, 8)}
            for j in range(i + 2, 8):
                low[j, i], low[j, i + 1] = e0[j] * d0, e1[j] * d1
            for j in range(i + 2, 8):
                for m in range(j, 8):
                    a[j, m] = a[j, m] - (low[j, i] * e0[m] + low[j, i + 1] * e1[m])
            w[i + 1] = w[i + 1] - l10 * w[i]
            for j in range(i + 2, 8):
                w[j] = w[j] - (low[j, i] * w[i] + low[j, i + 1] * w[i + 1])
            if more:
                c[i + 1] = c[i + 1] - l10 * c[i]
                for j in range(i + 2, 8):
                    c[j] = c[j] - (low[j, i] * c[i] + low[j, i + 1] * c[i + 1])
        z = [inverse_d[j] * w[j] for j in range(8)]
        if more:
            t = [c[j] * z[j] for j in range(8)]
            t = ((t[0] + t[1]) + (t[2] + t[3])) + ((t[4] + t[5]) + (t[6] + t[7]))
            ahead = jnp.where(inside, 0.0, following) - t
        solved = list(z)
        for j in range(7, -1, -1):
            for i in range(j):
                solved[i] = solved[i] - low[j, i] * solved[j]

        def together(parts):
            whole = parts[7]
            for i in range(7):
                whole = jnp.where(sub == i, parts[i], whole)
            return whole

        w_rows, z_rows, solved_rows = together(w), together(z), together(solved)
        left = jnp.where(inside, 0.0, jnp.where(lane < base, -w_rows, w_rows))
        update = product(left, z_rows)
        rows = [
            solved_rows if h == g else jnp.where(inside, 0.0, rows[h]) - update[8 * h : 8 * h + 8, :]
            for h in range(16)
        ]
        if more:
            rows[g + 1] = ahead
    return jnp.concatenate(rows, 0)


def kernel(
    tokens_all,
    inputs_ref, grads_ref, plan_ref, out_ref,
    data, given, taken, sums, in_y, in_z, next_z, next_y, last_in, part_z, part_y, last, result,
    load_sem, core_send, core_recv, y_send, y_recv, z_send, z_recv,
    z2_send, z2_recv, y2_send, y2_recv, x_send, x_recv,
    a1_send, a1_recv, b1_send, b1_recv, a2_send, a2_recv, b2_send, b2_recv,
    c_send, c_recv, out_sem,
):
    section = lax.axis_index("section")
    dp = lax.axis_index("dp")
    z, y, x, core = dp // 16, (dp // 4) % 4, (dp // 2) % 2, dp % 2

    def device(dz=0, dy=0, dx=0, dc=0):
        there = (((z + dz) % 4) * 4 + (y + dy) % 4) * 4 + ((x + dx) % 2) * 2 + (core + dc) % 2
        return (section, there)

    def pair_of(dy, dz):
        return ((y + dy) % 4) * 4 + (z + dz) % 4

    def load(ref, half, slot):
        pair = pair_of(*ORDER[slot])
        return pltpu.make_async_copy(
            ref.at[0, :, :, pl.ds(pl.multiple_of(pair * 256, 256), 256)],
            data.at[half, slot],
            load_sem.at[half, slot],
        )

    for mine, refs in ((0, (grads_ref, inputs_ref)), (1, (inputs_ref, grads_ref))):

        @pl.when(core == mine)
        def _():
            for half in range(2):
                for slot in range(PAIRS):
                    load(refs[half], half, slot).start()

    partners = [device(dc=1)]
    partners += [device(dy=d) for d in (1, 2, 3)] + [device(dz=d) for d in (1, 2, 3)]
    partners += [device(dx=1, dy=d) for d in range(4)] + [device(dx=1, dz=d) for d in (1, 2, 3)]
    barrier = pltpu.get_barrier_semaphore()
    for partner in partners:
        pl.semaphore_signal(barrier, inc=1, device_id=partner, device_id_type=MESH)

    row = lax.broadcasted_iota(jnp.int32, (HEAD, HEAD), 0)
    col = lax.broadcasted_iota(jnp.int32, (HEAD, HEAD), 1)

    def gram(half, slot):
        pair = pair_of(*ORDER[slot])
        whose = core if half else 1 - core
        factor = whose * 32 + pair * 2
        whole = data[half, slot].reshape(-1, 256)
        blocks = []
        for b in range(2):
            newest = plan_ref[0, factor + b, 1]
            own = slice(b * HEAD, (b + 1) * HEAD)
            right = [data[half, slot, 0, :, own]]
            for m in range(1, MICRO):
                kept = jnp.minimum(jnp.maximum(newest - (m - 1), 0), 1).astype(jnp.float32)
                kept = jnp.full((1, HEAD), kept, jnp.float32).astype(jnp.bfloat16)
                right.append(data[half, slot, m, :, own] * kept)
            blocks.append(
                lax.dot_general(
                    whole[:, own],
                    jnp.concatenate(right, 0),
                    (((0,), (0,)), ((), ())),
                    preferred_element_type=jnp.float32,
                )
            )
        packed = jnp.where(row >= col, blocks[0], blocks[1])
        diagonal = jnp.where(row == col, blocks[1], 0.0)
        return packed, jnp.sum(diagonal.reshape(16, 8, HEAD), axis=0)

    def remote(src, dst, send, recv, to):
        return pltpu.make_async_remote_copy(
            src_ref=src, dst_ref=dst, send_sem=send, recv_sem=recv, device_id=to, device_id_type=MESH
        )

    sent = []

    def start(copy):
        copy.start()
        sent.append(copy)

    def core_copy(slot):
        return remote(given.at[slot], taken.at[slot], core_send.at[slot], core_recv.at[slot], device(dc=1))

    for first in range(0, PAIRS, GROUP):
        for slot in range(first, first + GROUP):
            load(inputs_ref, 0, slot).wait()
        for slot in range(first, first + GROUP):
            packed, diagonal = gram(0, slot)
            given[slot, 0:HEAD, :] = packed
            given[slot, HEAD:PACK, :] = diagonal
        if first == 0:
            pl.semaphore_wait(barrier, len(partners))
        for slot in range(first, first + GROUP):
            start(core_copy(slot))

    def y_copy(dy, dz):
        slot = SLOT[dy, dz]
        i = (dy - 1) * 4 + dz
        return remote(sums.at[slot, 0:CUT], in_y.at[i], y_send.at[i], y_recv.at[i], device(dy=dy))

    def z_copy(dy, dz):
        slot = SLOT[dy, dz]
        i = (dz - 1) * 4 + dy
        return remote(sums.at[slot, CUT:PACK], in_z.at[i], z_send.at[i], z_recv.at[i], device(dz=dz))

    for first in range(0, PAIRS, GROUP):
        for slot in range(first, first + GROUP):
            load(inputs_ref, 1, slot).wait()
            core_copy(slot).wait_recv()
        for slot in range(first, first + GROUP):
            packed, diagonal = gram(1, slot)
            sums[slot, 0:HEAD, :] = packed + taken[slot, 0:HEAD, :]
            sums[slot, HEAD:PACK, :] = diagonal + taken[slot, HEAD:PACK, :]
        for slot in range(first, first + GROUP):
            dy, dz = ORDER[slot]
            if dy:
                start(y_copy(dy, dz))
            if dz:
                start(z_copy(dy, dz))

    def z2_copy(dz):
        return remote(part_z.at[dz], next_z.at[dz - 1], z2_send.at[dz - 1], z2_recv.at[dz - 1], device(dz=dz))

    def y2_copy(dy):
        return remote(part_y.at[dy], next_y.at[dy - 1], y2_send.at[dy - 1], y2_recv.at[dy - 1], device(dy=dy))

    for d in (2, 1, 3, 0):
        for o in (1, 2, 3):
            y_copy(o, d).wait_recv()
        part_z[d] = (sums[SLOT[0, d], 0:CUT] + in_y[d]) + (in_y[4 + d] + in_y[8 + d])
        if d:
            start(z2_copy(d))
        for o in (1, 2, 3):
            z_copy(d, o).wait_recv()
        part_y[d] = (sums[SLOT[d, 0], CUT:PACK] + in_z[d]) + (in_z[4 + d] + in_z[8 + d])
        if d:
            start(y2_copy(d))

    for d in (1, 3, 2):
        z2_copy(d).wait_recv()
        y2_copy(d).wait_recv()
    last[0:CUT] = (part_z[0] + next_z[0]) + (next_z[1] + next_z[2])
    last[CUT:PACK] = (part_y[0] + next_y[0]) + (next_y[1] + next_y[2])
    x_copy = remote(last, last_in, x_send.at[0], x_recv.at[0], device(dx=1))
    start(x_copy)
    x_copy.wait_recv()

    packed = last[0:HEAD] + last_in[0:HEAD]
    diagonal = jnp.sum(last[HEAD:PACK] + last_in[HEAD:PACK], axis=0, keepdims=True)
    second = x.astype(jnp.float32)
    triangle = jnp.where((row - col) * (1 - 2 * x) > 0, packed, 0.0)
    diagonal = second * diagonal + (1.0 - second) * packed
    total = triangle + triangle.T + jnp.where(row == col, diagonal, 0.0)
    newest = plan_ref[0, core * 32 + pair_of(0, 0) * 2 + x, 1]
    count = jnp.full((1, HEAD), (newest + 1).astype(jnp.float32), jnp.float32) * float(tokens_all)
    damped = total / count + jnp.where(row == col, DAMPING, 0.0)
    inverse = invert(damped)
    result[core, y, z, x] = inverse.astype(jnp.bfloat16)

    def a1_copy(dx, dy):
        i = dx * 4 + dy - 1
        here = result.at[core, y, z, x, 0:CUT]
        return remote(here, here, a1_send.at[i], a1_recv.at[i], device(dx=dx, dy=dy))

    def b1_copy(dx, dz):
        i = dx * 4 + dz - 1
        here = result.at[core, y, z, x, CUT:HEAD]
        return remote(here, here, b1_send.at[i], b1_recv.at[i], device(dx=dx, dz=dz))

    def a1_arrival(dx, dy):
        i = dx * 4 + dy - 1
        here = result.at[core, (y - dy) % 4, z, (x + dx) % 2, 0:CUT]
        return remote(here, here, a1_send.at[i], a1_recv.at[i], device(dx=dx, dy=dy))

    def b1_arrival(dx, dz):
        i = dx * 4 + dz - 1
        here = result.at[core, y, (z - dz) % 4, (x + dx) % 2, CUT:HEAD]
        return remote(here, here, b1_send.at[i], b1_recv.at[i], device(dx=dx, dz=dz))

    steps = [(0, 2), (0, 1), (0, 3), (1, 0), (1, 2), (1, 1), (1, 3)]
    for dx, d in steps:
        start(a1_copy(dx, d))
        start(b1_copy(dx, d))

    def a2_copy(dy, dz):
        i = dy * 3 + dz - 1
        here = result.at[core, (y - dy) % 4, z, :, 0:CUT]
        return remote(here, here, a2_send.at[i], a2_recv.at[i], device(dz=dz))

    def a2_arrival(dy, dz):
        i = dy * 3 + dz - 1
        here = result.at[core, (y - dy) % 4, (z - dz) % 4, :, 0:CUT]
        return remote(here, here, a2_send.at[i], a2_recv.at[i], device(dz=dz))

    def b2_copy(dz, dy):
        i = dz * 3 + dy - 1
        here = result.at[core, y, (z - dz) % 4, :, CUT:HEAD]
        return remote(here, here, b2_send.at[i], b2_recv.at[i], device(dy=dy))

    def b2_arrival(dz, dy):
        i = dz * 3 + dy - 1
        here = result.at[core, (y - dy) % 4, (z - dz) % 4, :, CUT:HEAD]
        return remote(here, here, b2_send.at[i], b2_recv.at[i], device(dy=dy))

    for d in (0, 1, 3, 2):
        for dx in (0, 1):
            if dx or d:
                a1_arrival(dx, d).wait_recv()
                b1_arrival(dx, d).wait_recv()
        for o in (2, 1, 3):
            start(a2_copy(d, o))
            start(b2_copy(d, o))

    def a3_copy(whose, dz):
        here = result.at[whose, :, (z - dz) % 4, :, 0:CUT]
        return remote(here, here, c_send.at[dz], c_recv.at[dz], device(dc=1))

    def b3_copy(whose, dy):
        here = result.at[whose, (y - dy) % 4, :, :, CUT:HEAD]
        return remote(here, here, c_send.at[4 + dy], c_recv.at[4 + dy], device(dc=1))

    start(a3_copy(core, 0))
    start(b3_copy(core, 0))
    for d in (1, 3, 2):
        for o in range(4):
            a2_arrival(o, d).wait_recv()
        start(a3_copy(core, d))
        for o in range(4):
            b2_arrival(o, d).wait_recv()
        start(b3_copy(core, d))

    def write(whose):
        return pltpu.make_async_copy(result.at[whose], out_ref.at[whose], out_sem.at[whose])

    mine = write(core)
    mine.start()
    for d in range(4):
        a3_copy(1 - core, d).wait_recv()
        b3_copy(1 - core, d).wait_recv()
    theirs = write(1 - core)
    theirs.start()
    for copy in sent:
        copy.wait_send()
    mine.wait()
    theirs.wait()


def shards(inputs, query_grads, plan):
    micro, tokens = inputs.shape[1], inputs.shape[2]
    members = lax.axis_size("dp")
    dma = pltpu.SemaphoreType.DMA
    f32, bf16 = jnp.float32, jnp.bfloat16
    vmem = pltpu.VMEM
    result = pl.pallas_call(
        functools.partial(kernel, tokens * members),
        out_shape=jax.ShapeDtypeStruct((2, 4, 4, 2, HEAD, HEAD), bf16),
        in_specs=[
            pl.BlockSpec(memory_space=pl.ANY),
            pl.BlockSpec(memory_space=pl.ANY),
            pl.BlockSpec(memory_space=pltpu.SMEM),
        ],
        out_specs=pl.BlockSpec(memory_space=pl.ANY),
        scratch_shapes=[
            vmem((2, PAIRS, micro, tokens, 256), bf16),
            vmem((PAIRS, PACK, HEAD), f32),
            vmem((PAIRS, PACK, HEAD), f32),
            vmem((PAIRS, PACK, HEAD), f32),
            vmem((12, CUT, HEAD), f32),
            vmem((12, PACK - CUT, HEAD), f32),
            vmem((3, CUT, HEAD), f32),
            vmem((3, PACK - CUT, HEAD), f32),
            vmem((PACK, HEAD), f32),
            vmem((4, CUT, HEAD), f32),
            vmem((4, PACK - CUT, HEAD), f32),
            vmem((PACK, HEAD), f32),
            vmem((2, 4, 4, 2, HEAD, HEAD), bf16),
            dma((2, PAIRS)),
            dma((PAIRS,)), dma((PAIRS,)),
            dma((12,)), dma((12,)), dma((12,)), dma((12,)),
            dma((3,)), dma((3,)), dma((3,)), dma((3,)),
            dma((1,)), dma((1,)),
            dma((7,)), dma((7,)), dma((7,)), dma((7,)),
            dma((12,)), dma((12,)), dma((12,)), dma((12,)),
            dma((8,)), dma((8,)),
            dma((2,)),
        ],
        compiler_params=pltpu.CompilerParams(
            collective_id=0, has_side_effects=True, vmem_limit_bytes=40 << 20
        ),
        name="factor_inverses",
    )(inputs, query_grads, plan)
    return result.reshape(1, 64, HEAD, HEAD)


def solution(mesh):
    in_specs = (
        P("section", None, "dp", None),
        P("section", None, "dp", None),
        P("section", None, None),
    )
    out_specs = P("section", None, None, None)
    return jax.shard_map(shards, mesh=mesh, in_specs=in_specs, out_specs=out_specs, check_vma=False)
```

time: 2250 us -> 55 us (0.02)
  other arithmetic: 1400 us -> 0 us
  waiting for transfers between devices: 697 us -> 0 us
  matrix products: 76.1 us -> 0 us
  Pallas kernels: 0 us -> 47.8 us
  blocking collectives: 25.6 us -> 0 us
    another operation x8 -> x0, other arithmetic: 1390 us -> none  [the longest x4 755 us: invert(): lower_factor = jnp.linalg.cholesky(damped)]
    psum x1 -> x0, waiting for transfers between devices: 650 us -> none  [shards(): factors = lax.psum(local_term, 'dp')]
    dot_general x6 -> x0, matrix products: 62.7 us -> none  [the longest x2 43.6 us: block_grams(): jnp.einsum('fm,mfij->fij', weights, gram_blocks, precision=lax.Precision....]
    pallas_call x0 -> x1, Pallas kernels: none -> 47.8 us  [shards(): pl.pallas_call(functools.partial(kernel, tokens * members), out_shape=jax...]
    all_to_all x1 -> x0, waiting for transfers between devices: 46.3 us -> none  [offload(): lax.all_to_all(packed, 'section', split_axis=0, concat_axis=0, tiled=True)]
    all_to_all x1 -> x0, blocking collectives: 25.6 us -> none  [offload(): lax.all_to_all(invert(lax.all_to_all(packed, 'section', split_axis=0, con...]
  transfers between devices with their start and end apart: 2 -> 0, of which waited for: 2 -> 0; matrix products, arithmetic and copies ran while one was open for 0% -> 0% of each run, Pallas kernels for 0% -> 0%
where the time goes in v1:
time: 55 us; the launch traced here: 54.8 us
  Pallas kernels  47.8 us (87%)
  local copies, waits for them, and re-layouts  7.06 us (13%)
    pallas_call x1, Pallas kernels, shards(): pl.pallas_call(functools.partial(kernel, tokens * members), out_shape=jax...  47.8 us
    unnamed x6, local copies, waits for them, and re-layouts  7.06 us

profile of v1, /device:TPU:1, one launch (start us, length us, event | category | flops | bytes accessed | tf_op | source)
XLA Modules:
  0.0 54.8 jit_solution(7888627863209495584)
XLA Ops:
  0.0 0.8 %copy.4.plan_ref = s32[1,64,2]{2,1,0:T(8,128)S(1)} copy(s32[1,64,2]{1,2,0:T(2,128)} %param.5) | data formatting | bytes 1024 | tf_op args[2]
  0.8 0.0 copy-start
  0.8 2.5 %copy-done = bf16[1,4,160,4096]{3,2,1,0:T(8,128)(2,1)S(1)} copy-done((bf16[1,4,160,4096]{3,2,1,0:T(8,128)(2,1)S(1)}, bf16[1,4,160,4096]{3,2,1,0:T(8,128)(2,1)}, u32[]{:S(2)}) %copy-start) | copy-done | bytes 5242904
  3.3 0.0 copy-start.1
  3.3 2.5 %copy-done.1 = bf16[1,4,160,4096]{3,2,1,0:T(8,128)(2,1)S(1)} copy-done((bf16[1,4,160,4096]{3,2,1,0:T(8,128)(2,1)S(1)}, bf16[1,4,160,4096]{3,2,1,0:T(8,128)(2,1)}, u32[]{:S(2)}) %copy-start.1) | copy-done | bytes 5242904
  5.7 47.8 %factor_inverses.1 = bf16[2,4,4,2,128,128]{5,4,3,2,1,0:T(8,128)(2,1)S(1)} custom-call(bf16[1,4,160,4096]{3,2,1,0:T(8,128)(2,1)S(1)} %copy-done, bf16[1,4,160,4096]{3,2,1,0:T(8,128)(2,1)S(1)} %copy-done.1, s32[1,64,2]{2,1,0:T(8,128)S(1)} %copy.4.plan_ref), custom_call_target="tpu_custom_call" | custom-call | tf_op jit(solution)/shard_map/factor_inverses/pallas_call | solution.py:371
  53.5 1.3 %copy.6 = bf16[1,64,128,128]{3,2,1,0:T(8,128)(2,1)} copy(bf16[1,64,128,128]{3,2,1,0:T(8,128)(2,1)S(1)} %bitcast.1) | data formatting | bytes 4194304
Async XLA Ops:
  0.8 2.5 %copy-start = (bf16[1,4,160,4096]{3,2,1,0:T(8,128)(2,1)S(1)}, bf16[1,4,160,4096]{3,2,1,0:T(8,128)(2,1)}, u32[]{:S(2)}) copy-start(bf16[1,4,160,4096]{3,2,1,0:T(8,128)(2,1)} %inputs_ref.1) | copy-start | bytes 15728644
  3.3 2.5 %copy-start.1 = (bf16[1,4,160,4096]{3,2,1,0:T(8,128)(2,1)S(1)}, bf16[1,4,160,4096]{3,2,1,0:T(8,128)(2,1)}, u32[]{:S(2)}) copy-start(bf16[1,4,160,4096]{3,2,1,0:T(8,128)(2,1)} %grads_ref.1) | copy-start | bytes 15728644

commit v2 on v1

--- a/solution.py
+++ b/solution.py
@@ -23,6 +23,7 @@
 )
 SLOT = {offset: slot for slot, offset in enumerate(ORDER)}
 GROUP = 4
+TURNS = ((0, 0), (0, 4), (1, 0), (0, 8), (1, 4), (0, 12), (1, 8), (1, 12))
 
 
 def split3(x):
@@ -114,12 +115,12 @@
 
 def kernel(
     tokens_all,
-    inputs_ref, grads_ref, plan_ref, out_ref,
-    data, given, taken, sums, in_y, in_z, next_z, next_y, last_in, part_z, part_y, last, result,
+    inputs_ref, grads_ref, plan_ref, result,
+    data, given, taken, sums, in_y, in_z, next_z, next_y, last_in, part_z, part_y, last, own,
     load_sem, core_send, core_recv, y_send, y_recv, z_send, z_recv,
     z2_send, z2_recv, y2_send, y2_recv, x_send, x_recv,
     a1_send, a1_recv, b1_send, b1_recv, a2_send, a2_recv, b2_send, b2_recv,
-    c_send, c_recv, out_sem,
+    c_send, c_recv, own_sem,
 ):
     section = lax.axis_index("section")
     dp = lax.axis_index("dp")
@@ -140,20 +141,20 @@
             load_sem.at[half, slot],
         )
 
-    for mine, refs in ((0, (grads_ref, inputs_ref)), (1, (inputs_ref, grads_ref))):
-
-        @pl.when(core == mine)
-        def _():
-            for half in range(2):
-                for slot in range(PAIRS):
-                    load(refs[half], half, slot).start()
-
     partners = [device(dc=1)]
     partners += [device(dy=d) for d in (1, 2, 3)] + [device(dz=d) for d in (1, 2, 3)]
-    partners += [device(dx=1, dy=d) for d in range(4)] + [device(dx=1, dz=d) for d in (1, 2, 3)]
+    partners += [device(dx=1)]
     barrier = pltpu.get_barrier_semaphore()
     for partner in partners:
         pl.semaphore_signal(barrier, inc=1, device_id=partner, device_id_type=MESH)
+
+    for mine, refs in ((0, (grads_ref, inputs_ref)), (1, (inputs_ref, grads_ref))):
+
+        @pl.when(core == mine)
+        def _():
+            for half, first in TURNS:
+                for slot in range(first, first + GROUP):
+                    load(refs[half], half, slot).start()
 
     row = lax.broadcasted_iota(jnp.int32, (HEAD, HEAD), 0)
     col = lax.broadcasted_iota(jnp.int32, (HEAD, HEAD), 1)
@@ -165,7 +166,7 @@
         whole = data[half, slot].reshape(-1, 256)
         blocks = []
         for b in range(2):
-            newest = plan_ref[0, factor + b, 1]
+            newest = plan_ref[0, 1, factor + b]
             own = slice(b * HEAD, (b + 1) * HEAD)
             right = [data[half, slot, 0, :, own]]
             for m in range(1, MICRO):
@@ -198,7 +199,17 @@
     def core_copy(slot):
         return remote(given.at[slot], taken.at[slot], core_send.at[slot], core_recv.at[slot], device(dc=1))
 
-    for first in range(0, PAIRS, GROUP):
+    def y_copy(dy, dz):
+        slot = SLOT[dy, dz]
+        i = (dy - 1) * 4 + dz
+        return remote(sums.at[slot, 0:CUT], in_y.at[i], y_send.at[i], y_recv.at[i], device(dy=dy))
+
+    def z_copy(dy, dz):
+        slot = SLOT[dy, dz]
+        i = (dz - 1) * 4 + dy
+        return remote(sums.at[slot, CUT:PACK], in_z.at[i], z_send.at[i], z_recv.at[i], device(dz=dz))
+
+    def work_other(first):
         for slot in range(first, first + GROUP):
             load(inputs_ref, 0, slot).wait()
         for slot in range(first, first + GROUP):
@@ -210,17 +221,7 @@
         for slot in range(first, first + GROUP):
             start(core_copy(slot))
 
-    def y_copy(dy, dz):
-        slot = SLOT[dy, dz]
-        i = (dy - 1) * 4 + dz
-        return remote(sums.at[slot, 0:CUT], in_y.at[i], y_send.at[i], y_recv.at[i], device(dy=dy))
-
-    def z_copy(dy, dz):
-        slot = SLOT[dy, dz]
-        i = (dz - 1) * 4 + dy
-        return remote(sums.at[slot, CUT:PACK], in_z.at[i], z_send.at[i], z_recv.at[i], device(dz=dz))
-
-    for first in range(0, PAIRS, GROUP):
+    def work_own(first):
         for slot in range(first, first + GROUP):
             load(inputs_ref, 1, slot).wait()
             core_copy(slot).wait_recv()
@@ -234,6 +235,9 @@
                 start(y_copy(dy, dz))
             if dz:
                 start(z_copy(dy, dz))
+
+    for half, first in TURNS:
+        (work_own if half else work_other)(first)
 
     def z2_copy(dz):
         return remote(part_z.at[dz], next_z.at[dz - 1], z2_send.at[dz - 1], z2_recv.at[dz - 1], device(dz=dz))
@@ -253,14 +257,19 @@
         if d:
             start(y2_copy(d))
 
+    def x_copy(i, where):
+        return remote(last.at[where], last_in.at[where], x_send.at[i], x_recv.at[i], device(dx=1))
+
     for d in (1, 3, 2):
         z2_copy(d).wait_recv()
+    last[0:CUT] = (part_z[0] + next_z[0]) + (next_z[1] + next_z[2])
+    start(x_copy(0, slice(0, CUT)))
+    for d in (1, 3, 2):
         y2_copy(d).wait_recv()
-    last[0:CUT] = (part_z[0] + next_z[0]) + (next_z[1] + next_z[2])
     last[CUT:PACK] = (part_y[0] + next_y[0]) + (next_y[1] + next_y[2])
-    x_copy = remote(last, last_in, x_send.at[0], x_recv.at[0], device(dx=1))
-    start(x_copy)
-    x_copy.wait_recv()
+    start(x_copy(1, slice(CUT, PACK)))
+    x_copy(0, slice(0, CUT)).wait_recv()
+    x_copy(1, slice(CUT, PACK)).wait_recv()
 
     packed = last[0:HEAD] + last_in[0:HEAD]
     diagonal = jnp.sum(last[HEAD:PACK] + last_in[HEAD:PACK], axis=0, keepdims=True)
@@ -268,21 +277,23 @@
     triangle = jnp.where((row - col) * (1 - 2 * x) > 0, packed, 0.0)
     diagonal = second * diagonal + (1.0 - second) * packed
     total = triangle + triangle.T + jnp.where(row == col, diagonal, 0.0)
-    newest = plan_ref[0, core * 32 + pair_of(0, 0) * 2 + x, 1]
+    newest = plan_ref[0, 1, core * 32 + pair_of(0, 0) * 2 + x]
     count = jnp.full((1, HEAD), (newest + 1).astype(jnp.float32), jnp.float32) * float(tokens_all)
     damped = total / count + jnp.where(row == col, DAMPING, 0.0)
     inverse = invert(damped)
-    result[core, y, z, x] = inverse.astype(jnp.bfloat16)
+    own[...] = inverse.astype(jnp.bfloat16)
+    place = pltpu.make_async_copy(own, result.at[core, y, z, x], own_sem.at[0])
+    place.start()
 
     def a1_copy(dx, dy):
         i = dx * 4 + dy - 1
         here = result.at[core, y, z, x, 0:CUT]
-        return remote(here, here, a1_send.at[i], a1_recv.at[i], device(dx=dx, dy=dy))
+        return remote(own.at[0:CUT], here, a1_send.at[i], a1_recv.at[i], device(dx=dx, dy=dy))
 
     def b1_copy(dx, dz):
         i = dx * 4 + dz - 1
         here = result.at[core, y, z, x, CUT:HEAD]
-        return remote(here, here, b1_send.at[i], b1_recv.at[i], device(dx=dx, dz=dz))
+        return remote(own.at[CUT:HEAD], here, b1_send.at[i], b1_recv.at[i], device(dx=dx, dz=dz))
 
     def a1_arrival(dx, dy):
         i = dx * 4 + dy - 1
@@ -294,39 +305,44 @@
         here = result.at[core, y, (z - dz) % 4, (x + dx) % 2, CUT:HEAD]
         return remote(here, here, b1_send.at[i], b1_recv.at[i], device(dx=dx, dz=dz))
 
-    steps = [(0, 2), (0, 1), (0, 3), (1, 0), (1, 2), (1, 1), (1, 3)]
-    for dx, d in steps:
+    def a2_copy(dx, dy, dz):
+        i = (dx * 4 + dy) * 3 + dz - 1
+        here = result.at[core, (y - dy) % 4, z, (x + dx) % 2, 0:CUT]
+        src = here if dx or dy else own.at[0:CUT]
+        return remote(src, here, a2_send.at[i], a2_recv.at[i], device(dz=dz))
+
+    def a2_arrival(dx, dy, dz):
+        i = (dx * 4 + dy) * 3 + dz - 1
+        here = result.at[core, (y - dy) % 4, (z - dz) % 4, (x + dx) % 2, 0:CUT]
+        return remote(here, here, a2_send.at[i], a2_recv.at[i], device(dz=dz))
+
+    def b2_copy(dx, dz, dy):
+        i = (dx * 4 + dz) * 3 + dy - 1
+        here = result.at[core, y, (z - dz) % 4, (x + dx) % 2, CUT:HEAD]
+        src = here if dx or dz else own.at[CUT:HEAD]
+        return remote(src, here, b2_send.at[i], b2_recv.at[i], device(dy=dy))
+
+    def b2_arrival(dx, dz, dy):
+        i = (dx * 4 + dz) * 3 + dy - 1
+        here = result.at[core, (y - dy) % 4, (z - dz) % 4, (x + dx) % 2, CUT:HEAD]
+        return remote(here, here, b2_send.at[i], b2_recv.at[i], device(dy=dy))
+
+    first_steps = [(0, 2), (1, 2), (1, 0), (1, 1), (1, 3), (0, 1), (0, 3)]
+    for dx, d in first_steps:
         start(a1_copy(dx, d))
         start(b1_copy(dx, d))
-
-    def a2_copy(dy, dz):
-        i = dy * 3 + dz - 1
-        here = result.at[core, (y - dy) % 4, z, :, 0:CUT]
-        return remote(here, here, a2_send.at[i], a2_recv.at[i], device(dz=dz))
-
-    def a2_arrival(dy, dz):
-        i = dy * 3 + dz - 1
-        here = result.at[core, (y - dy) % 4, (z - dz) % 4, :, 0:CUT]
-        return remote(here, here, a2_send.at[i], a2_recv.at[i], device(dz=dz))
-
-    def b2_copy(dz, dy):
-        i = dz * 3 + dy - 1
-        here = result.at[core, y, (z - dz) % 4, :, CUT:HEAD]
-        return remote(here, here, b2_send.at[i], b2_recv.at[i], device(dy=dy))
-
-    def b2_arrival(dz, dy):
-        i = dz * 3 + dy - 1
-        here = result.at[core, (y - dy) % 4, (z - dz) % 4, :, CUT:HEAD]
-        return remote(here, here, b2_send.at[i], b2_recv.at[i], device(dy=dy))
-
-    for d in (0, 1, 3, 2):
-        for dx in (0, 1):
-            if dx or d:
-                a1_arrival(dx, d).wait_recv()
-                b1_arrival(dx, d).wait_recv()
+    for o in (2, 1, 3):
+        start(a2_copy(0, 0, o))
+        start(b2_copy(0, 0, o))
+    arrivals = [(0, 1), (0, 3), (0, 2), (1, 0), (1, 1), (1, 3), (1, 2)]
+    for dx, d in arrivals:
+        a1_arrival(dx, d).wait_recv()
         for o in (2, 1, 3):
-            start(a2_copy(d, o))
-            start(b2_copy(d, o))
+            start(a2_copy(dx, d, o))
+        b1_arrival(dx, d).wait_recv()
+        for o in (2, 1, 3):
+            start(b2_copy(dx, d, o))
+    place.wait()
 
     def a3_copy(whose, dz):
         here = result.at[whose, :, (z - dz) % 4, :, 0:CUT]
@@ -339,27 +355,17 @@
     start(a3_copy(core, 0))
     start(b3_copy(core, 0))
     for d in (1, 3, 2):
-        for o in range(4):
-            a2_arrival(o, d).wait_recv()
+        for dx, o in [(0, 0)] + arrivals:
+            a2_arrival(dx, o, d).wait_recv()
         start(a3_copy(core, d))
-        for o in range(4):
-            b2_arrival(o, d).wait_recv()
+        for dx, o in [(0, 0)] + arrivals:
+            b2_arrival(dx, o, d).wait_recv()
         start(b3_copy(core, d))
-
-    def write(whose):
-        return pltpu.make_async_copy(result.at[whose], out_ref.at[whose], out_sem.at[whose])
-
-    mine = write(core)
-    mine.start()
     for d in range(4):
         a3_copy(1 - core, d).wait_recv()
         b3_copy(1 - core, d).wait_recv()
-    theirs = write(1 - core)
-    theirs.start()
     for copy in sent:
         copy.wait_send()
-    mine.wait()
-    theirs.wait()
 
 
 def shards(inputs, query_grads, plan):
@@ -370,7 +376,7 @@
     vmem = pltpu.VMEM
     result = pl.pallas_call(
         functools.partial(kernel, tokens * members),
-        out_shape=jax.ShapeDtypeStruct((2, 4, 4, 2, HEAD, HEAD), bf16),
+        out_shape=pltpu.VMEM((2, 4, 4, 2, HEAD, HEAD), bf16),
         in_specs=[
             pl.BlockSpec(memory_space=pl.ANY),
             pl.BlockSpec(memory_space=pl.ANY),
@@ -390,22 +396,22 @@
             vmem((4, CUT, HEAD), f32),
             vmem((4, PACK - CUT, HEAD), f32),
             vmem((PACK, HEAD), f32),
-            vmem((2, 4, 4, 2, HEAD, HEAD), bf16),
+            vmem((HEAD, HEAD), bf16),
             dma((2, PAIRS)),
             dma((PAIRS,)), dma((PAIRS,)),
             dma((12,)), dma((12,)), dma((12,)), dma((12,)),
             dma((3,)), dma((3,)), dma((3,)), dma((3,)),
-            dma((1,)), dma((1,)),
+            dma((2,)), dma((2,)),
             dma((7,)), dma((7,)), dma((7,)), dma((7,)),
-            dma((12,)), dma((12,)), dma((12,)), dma((12,)),
+            dma((24,)), dma((24,)), dma((24,)), dma((24,)),
             dma((8,)), dma((8,)),
-            dma((2,)),
+            dma((1,)),
         ],
         compiler_params=pltpu.CompilerParams(
-            collective_id=0, has_side_effects=True, vmem_limit_bytes=40 << 20
+            collective_id=0, has_side_effects=True, vmem_limit_bytes=54 << 20
         ),
         name="factor_inverses",
-    )(inputs, query_grads, plan)
+    )(inputs, query_grads, plan.transpose(0, 2, 1))
     return result.reshape(1, 64, HEAD, HEAD)
 
 

time: 55 us -> 45.2 us (0.82)
  local copies, waits for them, and re-layouts: 7.06 us -> 1.32 us
  Pallas kernels: 47.8 us -> 43.7 us
    unnamed x6 -> x1, local copies, waits for them, and re-layouts: 7.06 us -> 1.32 us
    pallas_call x1, Pallas kernels: 47.8 us -> 43.7 us  [shards(): pl.pallas_call(functools.partial(kernel, tokens * members), out_shape=plt...]
where the time goes in v2:
time: 45.2 us; the launch traced here: 45.1 us
  Pallas kernels  43.7 us (97%)
  local copies, waits for them, and re-layouts  1.32 us (3%)
    pallas_call x1, Pallas kernels, shards(): pl.pallas_call(functools.partial(kernel, tokens * members), out_shape=plt...  43.7 us
    unnamed x1, local copies, waits for them, and re-layouts  1.32 us

profile of v2, /device:TPU:1, one launch (start us, length us, event | category | flops | bytes accessed | tf_op | source)
XLA Modules:
  0.0 45.1 jit_solution(7942426654041045051)
XLA Ops:
  0.0 43.7 %factor_inverses.1 = bf16[2,4,4,2,128,128]{5,4,3,2,1,0:T(8,128)(2,1)S(1)} custom-call(bf16[1,4,160,4096]{3,2,1,0:T(8,128)(2,1)} %inputs_ref.1, bf16[1,4,160,4096]{3,2,1,0:T(8,128)(2,1)} %grads_ref.1, s32[1,2,64]{2,1,0:T(2,128)} %bitcast.3), custom_call_target="tpu_custom_call" | custom-call | tf_op jit(solution)/shard_map/factor_inverses/pallas_call | solution.py:377
  43.7 1.3 %copy.5 = bf16[1,64,128,128]{3,2,1,0:T(8,128)(2,1)} copy(bf16[1,64,128,128]{3,2,1,0:T(8,128)(2,1)S(1)} %bitcast.2) | data formatting | bytes 4194304

commit v3 on v2

--- a/solution.py
+++ b/solution.py
@@ -16,15 +16,18 @@
 MESH = pl.DeviceIdType.MESH
 
 ORDER = (
-    (2, 2), (2, 1), (1, 2), (2, 3),
-    (3, 2), (1, 1), (1, 3), (3, 1),
-    (3, 3), (2, 0), (0, 2), (1, 0),
-    (0, 1), (3, 0), (0, 3), (0, 0),
+    (2, 2), (2, 1), (1, 2),
+    (2, 3), (3, 2), (1, 1),
+    (1, 3), (3, 1), (3, 3),
+    (2, 0), (0, 2), (1, 0), (0, 1),
+    (3, 0), (0, 3), (0, 0),
 )
 SLOT = {offset: slot for slot, offset in enumerate(ORDER)}
-GROUP = 4
-TURNS = ((0, 0), (0, 4), (1, 0), (0, 8), (1, 4), (0, 12), (1, 8), (1, 12))
-
+GROUPS = (range(0, 3), range(3, 6), range(6, 9), range(9, 13), range(13, 16))
+TURNS = tuple(
+    (half, GROUPS[group])
+    for half, group in ((0, 0), (0, 1), (1, 0), (0, 2), (1, 1), (0, 3), (1, 2), (0, 4), (1, 3), (1, 4))
+)
 
 def split3(x):
     high = x.astype(jnp.bfloat16)
@@ -152,8 +155,8 @@
 
         @pl.when(core == mine)
         def _():
-            for half, first in TURNS:
-                for slot in range(first, first + GROUP):
+            for half, slots in TURNS:
+                for slot in slots:
                     load(refs[half], half, slot).start()
 
     row = lax.broadcasted_iota(jnp.int32, (HEAD, HEAD), 0)
@@ -209,35 +212,35 @@
         i = (dz - 1) * 4 + dy
         return remote(sums.at[slot, CUT:PACK], in_z.at[i], z_send.at[i], z_recv.at[i], device(dz=dz))
 
-    def work_other(first):
-        for slot in range(first, first + GROUP):
+    def work_other(slots):
+        for slot in slots:
             load(inputs_ref, 0, slot).wait()
-        for slot in range(first, first + GROUP):
+        for slot in slots:
             packed, diagonal = gram(0, slot)
             given[slot, 0:HEAD, :] = packed
             given[slot, HEAD:PACK, :] = diagonal
-        if first == 0:
+        if slots[0] == 0:
             pl.semaphore_wait(barrier, len(partners))
-        for slot in range(first, first + GROUP):
+        for slot in slots:
             start(core_copy(slot))
 
-    def work_own(first):
-        for slot in range(first, first + GROUP):
+    def work_own(slots):
+        for slot in slots:
             load(inputs_ref, 1, slot).wait()
             core_copy(slot).wait_recv()
-        for slot in range(first, first + GROUP):
+        for slot in slots:
             packed, diagonal = gram(1, slot)
             sums[slot, 0:HEAD, :] = packed + taken[slot, 0:HEAD, :]
             sums[slot, HEAD:PACK, :] = diagonal + taken[slot, HEAD:PACK, :]
-        for slot in range(first, first + GROUP):
+        for slot in slots:
             dy, dz = ORDER[slot]
             if dy:
                 start(y_copy(dy, dz))
             if dz:
                 start(z_copy(dy, dz))
 
-    for half, first in TURNS:
-        (work_own if half else work_other)(first)
+    for half, slots in TURNS:
+        (work_own if half else work_other)(slots)
 
     def z2_copy(dz):
         return remote(part_z.at[dz], next_z.at[dz - 1], z2_send.at[dz - 1], z2_recv.at[dz - 1], device(dz=dz))
@@ -344,26 +347,27 @@
             start(b2_copy(dx, d, o))
     place.wait()
 
-    def a3_copy(whose, dz):
-        here = result.at[whose, :, (z - dz) % 4, :, 0:CUT]
-        return remote(here, here, c_send.at[dz], c_recv.at[dz], device(dc=1))
-
-    def b3_copy(whose, dy):
-        here = result.at[whose, (y - dy) % 4, :, :, CUT:HEAD]
-        return remote(here, here, c_send.at[4 + dy], c_recv.at[4 + dy], device(dc=1))
-
-    start(a3_copy(core, 0))
-    start(b3_copy(core, 0))
-    for d in (1, 3, 2):
-        for dx, o in [(0, 0)] + arrivals:
-            a2_arrival(dx, o, d).wait_recv()
-        start(a3_copy(core, d))
-        for dx, o in [(0, 0)] + arrivals:
-            b2_arrival(dx, o, d).wait_recv()
-        start(b3_copy(core, d))
-    for d in range(4):
-        a3_copy(1 - core, d).wait_recv()
-        b3_copy(1 - core, d).wait_recv()
+    def a3_copy(whose, dx, dy):
+        i = dx * 4 + dy
+        here = result.at[whose, (y - dy) % 4, :, (x + dx) % 2, 0:CUT]
+        return remote(here, here, c_send.at[0, i], c_recv.at[0, i], device(dc=1))
+
+    def b3_copy(whose, dx, dz):
+        i = dx * 4 + dz
+        here = result.at[whose, :, (z - dz) % 4, (x + dx) % 2, CUT:HEAD]
+        return remote(here, here, c_send.at[1, i], c_recv.at[1, i], device(dc=1))
+
+    ways = [(0, 0)] + arrivals
+    for dx, d in ways:
+        for o in (1, 3, 2):
+            a2_arrival(dx, d, o).wait_recv()
+        start(a3_copy(core, dx, d))
+        for o in (1, 3, 2):
+            b2_arrival(dx, d, o).wait_recv()
+        start(b3_copy(core, dx, d))
+    for dx, d in ways:
+        a3_copy(1 - core, dx, d).wait_recv()
+        b3_copy(1 - core, dx, d).wait_recv()
     for copy in sent:
         copy.wait_send()
 
@@ -404,7 +408,7 @@
             dma((2,)), dma((2,)),
             dma((7,)), dma((7,)), dma((7,)), dma((7,)),
             dma((24,)), dma((24,)), dma((24,)), dma((24,)),
-            dma((8,)), dma((8,)),
+            dma((2, 8)), dma((2, 8)),
             dma((1,)),
         ],
         compiler_params=pltpu.CompilerParams(

time: 45.2 us -> 44.6 us (0.987)
  Pallas kernels: 43.7 us -> 43.1 us
    pallas_call x1, Pallas kernels: 43.7 us -> 43.1 us  [shards(): pl.pallas_call(functools.partial(kernel, tokens * members), out_shape=plt...]
where the time goes in v3:
time: 44.6 us; the launch traced here: 44.5 us
  Pallas kernels  43.1 us (97%)
  local copies, waits for them, and re-layouts  1.32 us (3%)
    pallas_call x1, Pallas kernels, shards(): pl.pallas_call(functools.partial(kernel, tokens * members), out_shape=plt...  43.1 us
    unnamed x1, local copies, waits for them, and re-layouts  1.32 us

profile of v3, /device:TPU:1, one launch (start us, length us, event | category | flops | bytes accessed | tf_op | source)
XLA Modules:
  0.0 44.5 jit_solution(8354623411299310952)
XLA Ops:
  0.0 43.1 %factor_inverses.1 = bf16[2,4,4,2,128,128]{5,4,3,2,1,0:T(8,128)(2,1)S(1)} custom-call(bf16[1,4,160,4096]{3,2,1,0:T(8,128)(2,1)} %inputs_ref.1, bf16[1,4,160,4096]{3,2,1,0:T(8,128)(2,1)} %grads_ref.1, s32[1,2,64]{2,1,0:T(2,128)} %bitcast.3), custom_call_target="tpu_custom_call" | custom-call | tf_op jit(solution)/shard_map/factor_inverses/pallas_call | solution.py:381
  43.1 1.3 %copy.5 = bf16[1,64,128,128]{3,2,1,0:T(8,128)(2,1)} copy(bf16[1,64,128,128]{3,2,1,0:T(8,128)(2,1)S(1)} %bitcast.2) | data formatting | bytes 4194304

commit v4 on v3

--- a/solution.py
+++ b/solution.py
@@ -49,7 +49,10 @@
     return jnp.broadcast_to(x, (8, HEAD))
 
 
-def invert(matrix):
+AHEAD = 3
+
+
+def invert(matrix, spot):
     lane = lax.broadcasted_iota(jnp.int32, (8, HEAD), 1)
     sub = lax.broadcasted_iota(jnp.int32, (8, HEAD), 0)
     rows = [matrix[8 * g : 8 * g + 8, :] for g in range(16)]
@@ -57,14 +60,15 @@
         base = 8 * g
         panel = rows[g]
         inside = (lane >= base) & (lane < base + 8)
-        columns = [spread(panel[:, base + j : base + j + 1]) for j in range(8)]
-        a = {(i, j): spread(columns[j][i : i + 1, :]) for i in range(8) for j in range(i, 8)}
         start = jnp.where(inside, jnp.where(lane - base == sub, 1.0, 0.0), panel)
-        w = [spread(start[j : j + 1, :]) for j in range(8)]
-        more = g + 1 < 16
-        if more:
-            following = rows[g + 1]
-            c = [spread(following[:, base + j : base + j + 1]) for j in range(8)]
+        here = (g % 2) * 9
+        for j in range(8):
+            spot[here + j] = spread(panel[:, base + j : base + j + 1])
+        spot[here + 8] = start
+        a = {(i, j): spread(spot[here + j, pl.ds(i, 1), :]) for i in range(8) for j in range(i, 8)}
+        w = [spread(spot[here + 8, pl.ds(j, 1), :]) for j in range(8)]
+        following = range(g + 1, min(16, g + 1 + AHEAD))
+        c = {h: [spread(rows[h][:, base + j : base + j + 1]) for j in range(8)] for h in following}
         low = {}
         inverse_d = [None] * 8
         for i in (0, 2, 4, 6):
@@ -81,18 +85,16 @@
             for j in range(i + 2, 8):
                 for m in range(j, 8):
                     a[j, m] = a[j, m] - (low[j, i] * e0[m] + low[j, i + 1] * e1[m])
-            w[i + 1] = w[i + 1] - l10 * w[i]
-            for j in range(i + 2, 8):
-                w[j] = w[j] - (low[j, i] * w[i] + low[j, i + 1] * w[i + 1])
-            if more:
-                c[i + 1] = c[i + 1] - l10 * c[i]
+            for v in [w, *c.values()]:
+                v[i + 1] = v[i + 1] - l10 * v[i]
                 for j in range(i + 2, 8):
-                    c[j] = c[j] - (low[j, i] * c[i] + low[j, i + 1] * c[i + 1])
+                    v[j] = v[j] - (low[j, i] * v[i] + low[j, i + 1] * v[i + 1])
         z = [inverse_d[j] * w[j] for j in range(8)]
-        if more:
-            t = [c[j] * z[j] for j in range(8)]
+        ahead = {}
+        for h in following:
+            t = [c[h][j] * z[j] for j in range(8)]
             t = ((t[0] + t[1]) + (t[2] + t[3])) + ((t[4] + t[5]) + (t[6] + t[7]))
-            ahead = jnp.where(inside, 0.0, following) - t
+            ahead[h] = jnp.where(inside, 0.0, rows[h]) - t
         solved = list(z)
         for j in range(7, -1, -1):
             for i in range(j):
@@ -111,15 +113,15 @@
             solved_rows if h == g else jnp.where(inside, 0.0, rows[h]) - update[8 * h : 8 * h + 8, :]
             for h in range(16)
         ]
-        if more:
-            rows[g + 1] = ahead
+        for h in following:
+            rows[h] = ahead[h]
     return jnp.concatenate(rows, 0)
 
 
 def kernel(
     tokens_all,
     inputs_ref, grads_ref, plan_ref, result,
-    data, given, taken, sums, in_y, in_z, next_z, next_y, last_in, part_z, part_y, last, own,
+    data, given, taken, sums, in_y, in_z, next_z, next_y, last_in, part_z, part_y, last, own, spot,
     load_sem, core_send, core_recv, y_send, y_recv, z_send, z_recv,
     z2_send, z2_recv, y2_send, y2_recv, x_send, x_recv,
     a1_send, a1_recv, b1_send, b1_recv, a2_send, a2_recv, b2_send, b2_recv,
@@ -161,6 +163,8 @@
 
     row = lax.broadcasted_iota(jnp.int32, (HEAD, HEAD), 0)
     col = lax.broadcasted_iota(jnp.int32, (HEAD, HEAD), 1)
+    half_row = lax.broadcasted_iota(jnp.int32, (CUT, HEAD), 0)
+    lane = lax.broadcasted_iota(jnp.int32, (CUT, HEAD), 1)
 
     def gram(half, slot):
         pair = pair_of(*ORDER[slot])
@@ -184,9 +188,13 @@
                     preferred_element_type=jnp.float32,
                 )
             )
-        packed = jnp.where(row >= col, blocks[0], blocks[1])
-        diagonal = jnp.where(row == col, blocks[1], 0.0)
-        return packed, jnp.sum(diagonal.reshape(16, 8, HEAD), axis=0)
+        folded = []
+        for block in blocks:
+            turned = pltpu.roll(block[CUT:], CUT, 1)
+            folded.append(jnp.where(lane <= half_row, block[:CUT], jnp.where(lane >= CUT, block[:CUT], turned)))
+        diagonals = jnp.where(lane == half_row, pltpu.roll(blocks[0][CUT:], CUT, 1), 0.0)
+        diagonals += jnp.where(lane == half_row + CUT, blocks[1][CUT:], 0.0)
+        return folded[0], folded[1], jnp.sum(diagonals.reshape(8, 8, HEAD), axis=0)
 
     def remote(src, dst, send, recv, to):
         return pltpu.make_async_remote_copy(
@@ -216,9 +224,10 @@
         for slot in slots:
             load(inputs_ref, 0, slot).wait()
         for slot in slots:
-            packed, diagonal = gram(0, slot)
-            given[slot, 0:HEAD, :] = packed
-            given[slot, HEAD:PACK, :] = diagonal
+            one, two, diagonals = gram(0, slot)
+            given[slot, 0:CUT] = one
+            given[slot, CUT:HEAD] = two
+            given[slot, HEAD:PACK] = diagonals
         if slots[0] == 0:
             pl.semaphore_wait(barrier, len(partners))
         for slot in slots:
@@ -229,9 +238,10 @@
             load(inputs_ref, 1, slot).wait()
             core_copy(slot).wait_recv()
         for slot in slots:
-            packed, diagonal = gram(1, slot)
-            sums[slot, 0:HEAD, :] = packed + taken[slot, 0:HEAD, :]
-            sums[slot, HEAD:PACK, :] = diagonal + taken[slot, HEAD:PACK, :]
+            one, two, diagonals = gram(1, slot)
+            sums[slot, 0:CUT] = one + taken[slot, 0:CUT]
+            sums[slot, CUT:HEAD] = two + taken[slot, CUT:HEAD]
+            sums[slot, HEAD:PACK] = diagonals + taken[slot, HEAD:PACK]
         for slot in slots:
             dy, dz = ORDER[slot]
             if dy:
@@ -260,30 +270,35 @@
         if d:
             start(y2_copy(d))
 
-    def x_copy(i, where):
-        return remote(last.at[where], last_in.at[where], x_send.at[i], x_recv.at[i], device(dx=1))
+    def rows_of(which):
+        return pl.ds(pl.multiple_of(which * CUT, CUT), CUT)
+
+    def x_copy(part):
+        src, dst = ((rows_of(1 - x), slice(0, CUT)), (slice(HEAD, PACK), slice(CUT, CUT + 8)))[part]
+        return remote(last.at[src], last_in.at[dst], x_send.at[part], x_recv.at[part], device(dx=1))
 
     for d in (1, 3, 2):
         z2_copy(d).wait_recv()
+        y2_copy(d).wait_recv()
     last[0:CUT] = (part_z[0] + next_z[0]) + (next_z[1] + next_z[2])
-    start(x_copy(0, slice(0, CUT)))
-    for d in (1, 3, 2):
-        y2_copy(d).wait_recv()
     last[CUT:PACK] = (part_y[0] + next_y[0]) + (next_y[1] + next_y[2])
-    start(x_copy(1, slice(CUT, PACK)))
-    x_copy(0, slice(0, CUT)).wait_recv()
-    x_copy(1, slice(CUT, PACK)).wait_recv()
-
-    packed = last[0:HEAD] + last_in[0:HEAD]
-    diagonal = jnp.sum(last[HEAD:PACK] + last_in[HEAD:PACK], axis=0, keepdims=True)
+    start(x_copy(0))
+    start(x_copy(1))
+    x_copy(0).wait_recv()
+    x_copy(1).wait_recv()
+
+    folded = last[rows_of(x)] + last_in[0:CUT]
+    diagonals = jnp.sum(last[HEAD:PACK] + last_in[CUT : CUT + 8], axis=0, keepdims=True)
     second = x.astype(jnp.float32)
-    triangle = jnp.where((row - col) * (1 - 2 * x) > 0, packed, 0.0)
-    diagonal = second * diagonal + (1.0 - second) * packed
-    total = triangle + triangle.T + jnp.where(row == col, diagonal, 0.0)
+    diagonals = second * diagonals + (1.0 - second) * pltpu.roll(jnp.broadcast_to(diagonals, (8, HEAD)), CUT, 1)[0:1]
+    unfolded = jnp.concatenate([folded, pltpu.roll(folded, CUT, 1)], 0)
+    stored = ((row < CUT) & ((col >= CUT) | (col < row))) | ((row >= CUT) & (col > row))
+    triangle = jnp.where(stored, unfolded, 0.0)
+    total = triangle + triangle.T + jnp.where(row == col, jnp.where(row < CUT, unfolded, diagonals), 0.0)
     newest = plan_ref[0, 1, core * 32 + pair_of(0, 0) * 2 + x]
     count = jnp.full((1, HEAD), (newest + 1).astype(jnp.float32), jnp.float32) * float(tokens_all)
     damped = total / count + jnp.where(row == col, DAMPING, 0.0)
-    inverse = invert(damped)
+    inverse = invert(damped, spot)
     own[...] = inverse.astype(jnp.bfloat16)
     place = pltpu.make_async_copy(own, result.at[core, y, z, x], own_sem.at[0])
     place.start()
@@ -396,11 +411,12 @@
             vmem((12, PACK - CUT, HEAD), f32),
             vmem((3, CUT, HEAD), f32),
             vmem((3, PACK - CUT, HEAD), f32),
-            vmem((PACK, HEAD), f32),
+            vmem((CUT + 8, HEAD), f32),
             vmem((4, CUT, HEAD), f32),
             vmem((4, PACK - CUT, HEAD), f32),
             vmem((PACK, HEAD), f32),
             vmem((HEAD, HEAD), bf16),
+            vmem((18, 8, HEAD), f32),
             dma((2, PAIRS)),
             dma((PAIRS,)), dma((PAIRS,)),
             dma((12,)), dma((12,)), dma((12,)), dma((12,)),

time: 44.6 us -> 42.7 us (0.957)
  Pallas kernels: 43.1 us -> 41.3 us
    pallas_call x1, Pallas kernels: 43.1 us -> 41.3 us  [shards(): pl.pallas_call(functools.partial(kernel, tokens * members), out_shape=plt...]
where the time goes in v4:
time: 42.7 us; the launch traced here: 42.6 us
  Pallas kernels  41.3 us (97%)
  local copies, waits for them, and re-layouts  1.32 us (3%)
    pallas_call x1, Pallas kernels, shards(): pl.pallas_call(functools.partial(kernel, tokens * members), out_shape=plt...  41.3 us
    unnamed x1, local copies, waits for them, and re-layouts  1.32 us

profile of v4, /device:TPU:1, one launch (start us, length us, event | category | flops | bytes accessed | tf_op | source)
XLA Modules:
  0.0 42.6 jit_solution(8851622804582003415)
XLA Ops:
  0.0 41.3 %factor_inverses.1 = bf16[2,4,4,2,128,128]{5,4,3,2,1,0:T(8,128)(2,1)S(1)} custom-call(bf16[1,4,160,4096]{3,2,1,0:T(8,128)(2,1)} %inputs_ref.1, bf16[1,4,160,4096]{3,2,1,0:T(8,128)(2,1)} %grads_ref.1, s32[1,2,64]{2,1,0:T(2,128)} %bitcast.3), custom_call_target="tpu_custom_call" | custom-call | tf_op jit(solution)/shard_map/factor_inverses/pallas_call | solution.py:396
  41.3 1.3 %copy.5 = bf16[1,64,128,128]{3,2,1,0:T(8,128)(2,1)} copy(bf16[1,64,128,128]{3,2,1,0:T(8,128)(2,1)S(1)} %bitcast.2) | data formatting | bytes 4194304

commit v5 on v4

--- a/solution.py
+++ b/solution.py
@@ -236,13 +236,14 @@
     def work_own(slots):
         for slot in slots:
             load(inputs_ref, 1, slot).wait()
+        for slot in slots:
+            one, two, diagonals = gram(1, slot)
+            sums[slot, 0:CUT] = one
+            sums[slot, CUT:HEAD] = two
+            sums[slot, HEAD:PACK] = diagonals
+        for slot in slots:
             core_copy(slot).wait_recv()
-        for slot in slots:
-            one, two, diagonals = gram(1, slot)
-            sums[slot, 0:CUT] = one + taken[slot, 0:CUT]
-            sums[slot, CUT:HEAD] = two + taken[slot, CUT:HEAD]
-            sums[slot, HEAD:PACK] = diagonals + taken[slot, HEAD:PACK]
-        for slot in slots:
+            sums[slot] += taken[slot]
             dy, dz = ORDER[slot]
             if dy:
                 start(y_copy(dy, dz))

time: 42.7 us -> 42.8 us (level)
  no operation moved by 1% of the time
where the time goes in v5:
time: 42.8 us; the launch traced here: 42.7 us
  Pallas kernels  41.3 us (96%)
  local copies, waits for them, and re-layouts  1.32 us (3%)
    pallas_call x1, Pallas kernels, shards(): pl.pallas_call(functools.partial(kernel, tokens * members), out_shape=plt...  41.3 us
    unnamed x1, local copies, waits for them, and re-layouts  1.32 us

profile of v5, /device:TPU:1, one launch (start us, length us, event | category | flops | bytes accessed | tf_op | source)
XLA Modules:
  0.0 42.7 jit_solution(8625401520965847426)
XLA Ops:
  0.0 41.3 %factor_inverses.1 = bf16[2,4,4,2,128,128]{5,4,3,2,1,0:T(8,128)(2,1)S(1)} custom-call(bf16[1,4,160,4096]{3,2,1,0:T(8,128)(2,1)} %inputs_ref.1, bf16[1,4,160,4096]{3,2,1,0:T(8,128)(2,1)} %grads_ref.1, s32[1,2,64]{2,1,0:T(2,128)} %bitcast.3), custom_call_target="tpu_custom_call" | custom-call | tf_op jit(solution)/shard_map/factor_inverses/pallas_call | solution.py:397
  41.3 1.3 %copy.5 = bf16[1,64,128,128]{3,2,1,0:T(8,128)(2,1)} copy(bf16[1,64,128,128]{3,2,1,0:T(8,128)(2,1)S(1)} %bitcast.2) | data formatting | bytes 4194304
